TPU v7x, 32 devices: a whole 2x2x4 slice. The times are simulated.
32 devices in a mesh: seq: 16 (over z, y, x), head: 2 (over core).
Axes of the slice: x: 2, y: 2, z: 4, core: 2. Of those that a mesh axis runs over, the one named last changes fastest.
Arguments:
- queries: bfloat16 [8192, 4096], P('seq', 'head'), may hold values from -64 to 64
- keys: bfloat16 [8192, 2048], P('seq', 'head'), may hold values from -20 to 20
- values: bfloat16 [8192, 2048], P('seq', 'head'), may hold values from -6 to 6
- start_basis: float32 [16, 128, 64], P('head'), may hold values from -6 to 6
- out_weight: bfloat16 [4096, 2688], P('head'), may hold values from -0.09375 to 0.09375
Outputs:
- lowrank_attn: bfloat16 [8192, 4096], P('seq', 'head')
- deviation: bfloat16 [8192, 2688], P(('seq', 'head'))
All inputs are finite; a program needn't handle non-finite values.
Results may differ from a plain program's by a relative error of at most 0.029.
Values may be sent and summed in bfloat16 or wider, within the bound.
A program may use at most 192 MiB of HBM per device.

v0:
```python
import jax
import jax.numpy as jnp
from jax import lax
from jax.sharding import PartitionSpec as P

HQ = 32
HK = 16
HD = 128
QSCALE = 168
W = 1024
SWEEPS = 8


HIGHEST = lax.Precision.HIGHEST
NEGLIGIBLE = -1e30


def from_behind(array, axis, by):
    peers = lax.axis_size(axis)
    pairs = [(i, i + by) for i in range(peers) if 0 <= i + by < peers]
    return lax.ppermute(array, axis, pairs)


def orthonormal(columns):
    inner_prod = jnp.einsum("hcr,hcq->hrq", columns, columns, precision=HIGHEST)
    factor_low = jnp.linalg.cholesky(inner_prod)

    def solve_one(factor, column):
        return jax.scipy.linalg.solve_triangular(factor, column.T, lower=True).T

    return jax.vmap(solve_one)(factor_low, columns)


def attend(query_rows, key_rows, value_rows, first_pos, score_scale):
    row_count = query_rows.shape[0]
    key_span = key_rows.shape[0]
    query_pos = first_pos + jnp.arange(row_count, dtype=jnp.int32)
    key_pos = first_pos + row_count - key_span + jnp.arange(key_span, dtype=jnp.int32)
    allowed = (
        (key_pos[None, :] >= 0)
        & (key_pos[None, :] <= query_pos[:, None])
        & (query_pos[:, None] - key_pos[None, :] < W)
    )
    scores = (
        jnp.einsum("thgd,shd->hgts", query_rows, key_rows, preferred_element_type=jnp.float32)
        * score_scale
    )
    scores = jnp.where(allowed, scores, NEGLIGIBLE)
    row_peak = jnp.max(scores, axis=-1, keepdims=True)
    raised = jnp.exp(scores - row_peak)
    weights = (raised / jnp.sum(raised, axis=-1, keepdims=True)).astype(jnp.bfloat16)
    return jnp.einsum("hgts,shd->thgd", weights, value_rows, preferred_element_type=jnp.float32)


def shards(queries, keys, values, start_basis, out_weight):
    tok_rows = keys.shape[0]
    kv_local = keys.shape[1] // HD
    group_q = HQ // HK
    prior_count = W // tok_rows
    first_pos = lax.axis_index("seq") * tok_rows
    score_scale = QSCALE ** (-0.5)
    key_heads = keys.reshape(tok_rows, kv_local, HD)
    paired = jnp.stack([keys, values])
    pieces = []
    for distance in range(prior_count, 0, -1):
        pieces.append(from_behind(paired, "seq", distance))
    window_kv = jnp.concatenate(pieces + [paired], axis=1)
    window_keys = window_kv[0].reshape(-1, kv_local, HD)
    window_vals = window_kv[1].reshape(-1, kv_local, HD)
    basis = start_basis
    local_gram = jnp.einsum(
        "thc,thd->hcd", key_heads, key_heads, preferred_element_type=jnp.float32
    )
    key_gram = lax.psum(local_gram, "seq")
    for sweep in range(SWEEPS):
        basis = orthonormal(jnp.einsum("hcd,hdr->hcr", key_gram, basis, precision=HIGHEST))
    basis_half = basis.astype(jnp.bfloat16)
    query_heads = queries.reshape(tok_rows, kv_local, group_q, HD)
    query_low = jnp.einsum(
        "thgc,hcr->thgr", query_heads, basis_half, preferred_element_type=jnp.float32
    ).astype(jnp.bfloat16)
    key_low = jnp.einsum(
        "shc,hcr->shr", window_keys, basis_half, preferred_element_type=jnp.float32
    ).astype(jnp.bfloat16)
    exact = attend(query_heads, window_keys, window_vals, first_pos, score_scale)
    approx = attend(query_low, key_low, window_vals, first_pos, score_scale)
    lowrank_attn = approx.astype(jnp.bfloat16).reshape(tok_rows, -1)
    gap_rows = (exact - approx).astype(jnp.bfloat16).reshape(tok_rows, -1)
    deviation = lax.psum_scatter(
        jnp.dot(gap_rows, out_weight, preferred_element_type=jnp.float32).astype(jnp.bfloat16),
        "head",
        scatter_dimension=0,
        tiled=True,
    )
    return (lowrank_attn, deviation)


def solution(mesh):
    placed = (
        P("seq", "head"),
        P("seq", "head"),
        P("seq", "head"),
        P("head", None, None),
        P("head", None),
    )
    return jax.shard_map(
        shards,
        mesh=mesh,
        in_specs=placed,
        out_specs=(P("seq", "head"), P(("seq", "head"), None)),
        check_vma=False,
    )
```

profile of v0, /device:TPU:13, one launch (start us, length us, event | category | flops | bytes accessed | tf_op | source)
XLA Modules:
  0.0 1064.3 jit_solution(13927120682030233892)
XLA Ops:
  7.2 1.5 copy.42
  8.8 1.5 copy.41
  10.3 1.5 pad_maximum_fusion
  11.8 3.1 collective-permute-start.1
  14.9 3.1 collective-permute-start
  18.1 1.3 fusion.33
  19.6 4.4 reshape.42
  24.0 1.9 fusion.16
  26.0 182.6 %all-reduce.2.cloned.1.call-done = f32[8,128,128]{2,1,0:T(8,128)} async-done(((f32[8,128,128]{2,1,0:T(8,128)}), f32[8,128,128]{2,1,0:T(8,128)}) %all-reduce.2.cloned.1.call-update) | async-done | bytes 524304 | tf_op jit(solution)/shard_map/psum | solution.py:74
  208.6 2.2 fusion.80
  211.5 0.7 fusion.66
  212.2 47.6 %custom-call.20 = f32[8,64,64]{2,1,0:T(8,128)S(1)} custom-call(f32[8,64,64]{2,1,0:T(8,128)} %fusion.66), custom_call_target="Cholesky" | custom-call | tf_op jit(solution)/shard_map/jit(cholesky)/cholesky | solution.py:26
  260.1 39.3 %custom-call.21 = f32[8,1,64,64]{2,3,1,0:T(8,128)S(1)} custom-call(f32[8,1,64,64]{3,2,1,0:T(8,128)S(1)} %select_bitcast_fusion.7), custom_call_target="InvertDiagBlocksLowerTriangular" | custom-call | tf_op jit(solution)/shard_map/vmap(jit(_solve_triangular))/triangular_solve | solution.py:29
  299.5 0.6 fusion.63
  300.1 1.1 fusion.82
  301.2 0.5 fusion.83
  301.9 0.7 fusion.62
  302.6 47.6 %custom-call.22 = f32[8,64,64]{2,1,0:T(8,128)S(1)} custom-call(f32[8,64,64]{2,1,0:T(8,128)} %fusion.62), custom_call_target="Cholesky" | custom-call | tf_op jit(solution)/shard_map/jit(cholesky)/cholesky | solution.py:26
  350.5 39.3 %custom-call.23 = f32[8,1,64,64]{2,3,1,0:T(8,128)S(1)} custom-call(f32[8,1,64,64]{3,2,1,0:T(8,128)S(1)} %select_bitcast_fusion.6), custom_call_target="InvertDiagBlocksLowerTriangular" | custom-call | tf_op jit(solution)/shard_map/vmap(jit(_solve_triangular))/triangular_solve | solution.py:29
  389.8 0.6 fusion.59
  390.4 1.1 fusion.84
  392.3 0.7 fusion.58
  393.0 47.6 %custom-call.24 = f32[8,64,64]{2,1,0:T(8,128)S(1)} custom-call(f32[8,64,64]{2,1,0:T(8,128)} %fusion.58), custom_call_target="Cholesky" | custom-call | tf_op jit(solution)/shard_map/jit(cholesky)/cholesky | solution.py:26
  440.9 39.8 %custom-call.25 = f32[8,1,64,64]{2,3,1,0:T(8,128)S(1)} custom-call(f32[8,1,64,64]{3,2,1,0:T(8,128)S(1)} %select_bitcast_fusion.5), custom_call_target="InvertDiagBlocksLowerTriangular" | custom-call | tf_op jit(solution)/shard_map/vmap(jit(_solve_triangular))/triangular_solve | solution.py:29
  480.7 0.6 fusion.55
  481.3 1.1 fusion.86
  483.1 0.7 fusion.54
  483.8 47.6 %custom-call.26 = f32[8,64,64]{2,1,0:T(8,128)S(1)} custom-call(f32[8,64,64]{2,1,0:T(8,128)} %fusion.54), custom_call_target="Cholesky" | custom-call | tf_op jit(solution)/shard_map/jit(cholesky)/cholesky | solution.py:26
  531.7 39.3 %custom-call.27 = f32[8,1,64,64]{2,3,1,0:T(8,128)S(1)} custom-call(f32[8,1,64,64]{3,2,1,0:T(8,128)S(1)} %select_bitcast_fusion.4), custom_call_target="InvertDiagBlocksLowerTriangular" | custom-call | tf_op jit(solution)/shard_map/vmap(jit(_solve_triangular))/triangular_solve | solution.py:29
  571.0 0.6 fusion.51
  571.6 1.1 fusion.88
  572.7 0.5 fusion.89
  573.4 0.7 fusion.50
  574.2 47.6 %custom-call.28 = f32[8,64,64]{2,1,0:T(8,128)S(1)} custom-call(f32[8,64,64]{2,1,0:T(8,128)} %fusion.50), custom_call_target="Cholesky" | custom-call | tf_op jit(solution)/shard_map/jit(cholesky)/cholesky | solution.py:26
  622.1 39.3 %custom-call.29 = f32[8,1,64,64]{2,3,1,0:T(8,128)S(1)} custom-call(f32[8,1,64,64]{3,2,1,0:T(8,128)S(1)} %select_bitcast_fusion.3), custom_call_target="InvertDiagBlocksLowerTriangular" | custom-call | tf_op jit(solution)/shard_map/vmap(jit(_solve_triangular))/triangular_solve | solution.py:29
  661.4 0.6 fusion.47
  662.0 1.1 fusion.90
  663.1 0.5 fusion.91
  663.8 0.7 fusion.46
  664.5 47.6 %custom-call.30 = f32[8,64,64]{2,1,0:T(8,128)S(1)} custom-call(f32[8,64,64]{2,1,0:T(8,128)} %fusion.46), custom_call_target="Cholesky" | custom-call | tf_op jit(solution)/shard_map/jit(cholesky)/cholesky | solution.py:26
  712.4 39.5 %custom-call.31 = f32[8,1,64,64]{2,3,1,0:T(8,128)S(1)} custom-call(f32[8,1,64,64]{3,2,1,0:T(8,128)S(1)} %select_bitcast_fusion.2), custom_call_target="InvertDiagBlocksLowerTriangular" | custom-call | tf_op jit(solution)/shard_map/vmap(jit(_solve_triangular))/triangular_solve | solution.py:29
  751.9 0.6 fusion.43
  752.5 1.1 fusion.92
  754.3 0.7 fusion.42
  755.1 47.6 %custom-call.32 = f32[8,64,64]{2,1,0:T(8,128)S(1)} custom-call(f32[8,64,64]{2,1,0:T(8,128)} %fusion.42), custom_call_target="Cholesky" | custom-call | tf_op jit(solution)/shard_map/jit(cholesky)/cholesky | solution.py:26
  803.0 39.3 %custom-call.33 = f32[8,1,64,64]{2,3,1,0:T(8,128)S(1)} custom-call(f32[8,1,64,64]{3,2,1,0:T(8,128)S(1)} %select_bitcast_fusion.1), custom_call_target="InvertDiagBlocksLowerTriangular" | custom-call | tf_op jit(solution)/shard_map/vmap(jit(_solve_triangular))/triangular_solve | solution.py:29
  842.3 0.6 fusion.39
  842.9 1.1 fusion.94
  844.0 0.5 fusion.95
  844.7 46.9 %custom-call.34 = f32[8,64,64]{2,1,0:T(8,128)S(1)} custom-call(f32[8,64,64]{2,1,0:T(8,128)S(1)} %fusion.38), custom_call_target="Cholesky" | custom-call | tf_op jit(solution)/shard_map/jit(cholesky)/cholesky | solution.py:26
  891.9 39.3 %custom-call.35 = f32[8,1,64,64]{2,3,1,0:T(8,128)S(1)} custom-call(f32[8,1,64,64]{3,2,1,0:T(8,128)S(1)} %select_bitcast_fusion), custom_call_target="InvertDiagBlocksLowerTriangular" | custom-call | tf_op jit(solution)/shard_map/vmap(jit(_solve_triangular))/triangular_solve | solution.py:29
  931.2 0.6 convolution_convert_fusion.2
  931.9 3.6 fusion.30
  935.5 3.1 maximum_maximum_fusion
  938.5 2.0 fusion.72
  940.6 1.7 fusion.17
  942.3 23.6 %fusion.75 = (f32[8,2,512]{2,1,0:T(2,128)S(1)}, f32[8,2,512,1536]{2,3,1,0:T(8,128)}) fusion(pred[512,1536]{0,1:T(8,128)(4,1)} %fusion.16, bf16[1536,8,128,1]{0,2,3,1:T(8,128)(2,1)S(1)} %bitcast.201, bf16[512,8,2,128]{3,2,1,0:T(2,128)(2,1)} %reshape.42), kind=kOutput, calls=%fused_computation.115 | convolution fusion | flops 3271558656 | bytes 56393728 | tf_op jit(solution)/shard_map/sub | solution.py:50
  965.9 26.4 %fusion.73 = (f32[8,2,512]{2,1,0:T(2,128)S(1)}, f32[8,2,512,1536]{2,3,1,0:T(8,128)}) fusion(pred[512,1536]{0,1:T(8,128)(4,1)} %fusion.16, bf16[1536,8,64,1]{0,2,3,1:T(8,128)(2,1)} %fusion.17, bf16[512,8,2,64]{0,3,2,1:T(8,128)(2,1)} %fusion.30), kind=kOutput, calls=%fused_computation.113 | convolution fusion | flops 1660945920 | bytes 53772288 | tf_op jit(solution)/shard_map/sub | solution.py:50
  992.3 19.8 %fusion.74 = (bf16[8,128,2,512]{3,1,2,0:T(8,128)(2,1)}, f32[8,128,2,512]{3,1,2,0:T(8,128)}) fusion(bf16[1536,8,128,1]{0,2,3,1:T(8,128)(2,1)S(1)} %bitcast.206, f32[8,2,512,1536]{2,3,1,0:T(8,128)} %get-tuple-element.13, f32[8,2,512]{2,1,0:T(2,128)S(1)} %get-tuple-element.12), kind=kOutput, calls=%fused_computation.114 | convolution fusion | flops 3247439872 | bytes 59801600 | tf_op jit(solution)/shard_map/hgts,shd->thgd/dot_general | solution.py:52
  1012.2 20.1 %subtract_convert_fusion = bf16[8,128,2,512]{3,1,2,0:T(8,128)(2,1)} fusion(f32[8,128,2,512]{3,1,2,0:T(8,128)} %get-tuple-element.15, bf16[1536,8,128,1]{0,2,3,1:T(8,128)(2,1)S(1)} %bitcast.207, f32[8,2,512,1536]{2,3,1,0:T(8,128)} %get-tuple-element.17, f32[8,2,512]{2,1,0:T(2,128)S(1)} %get-tuple-element.16), kind=kOutput, calls=%fused_computation.22 | convolution fusion | flops 3248488448 | bytes 59801600 | tf_op jit(solution)/shard_map/hgts,shd->thgd/dot_general | solution.py:52
  1032.2 12.0 %convolution_convert_fusion = bf16[512,2688]{1,0:T(8,128)(2,1)} fusion(bf16[512,2048]{0,1:T(8,128)(2,1)} %bitcast.209, bf16[2048,2688]{1,0:T(8,128)(2,1)} %param.12), kind=kOutput, calls=%fused_computation.21 | convolution fusion | flops 5638520832 | bytes 15859712 | tf_op jit(solution)/shard_map/dot_general | solution.py:90
  1044.2 1.6 copy-done.4
  1045.8 2.4 copy.67
  1048.2 8.9 reduce-scatter.2.cloned.1.call-done
  (59 shorter events, 5.5 us)
Async XLA Ops:
  7.2 201.4 %copy-start = (f32[8,128,64]{1,2,0:T(8,128)S(1)}, f32[8,128,64]{1,2,0:T(8,128)}, u32[]{:S(2)}) copy-start(f32[8,128,64]{1,2,0:T(8,128)} %param.11) | copy-start | bytes 786436
  7.2 201.4 %all-reduce.2.cloned.1.call-start = ((), (), s32[]{:S(2)}) async-start(), calls=%async_computation.1 | async-start | bytes 1048576 | tf_op jit(solution)/shard_map/psum | solution.py:74
  10.3 7.8 copy-start.5
  11.8 923.7 %collective-permute-start.1 = (bf16[2,512,1024]{1,2,0:T(8,128)(2,1)}, bf16[2,512,1024]{1,2,0:T(8,128)(2,1)}, u32[]{:S(2)}, u32[]{:S(2)}) collective-permute-start(bf16[2,512,1024]{1,2,0:T(8,128)(2,1)} %pad_maximum_fusion), channel_id=1, source_target_pairs={{0,2},{2,4},{4,6},{6,8},{8,10},{10,12},{12,14},{14,16},{16,18},{18... | collective-permute-start | bytes 6291464 | tf_op jit(solution)/shard_map/ppermute | solution.py:21
  14.9 920.6 %collective-permute-start = (bf16[2,512,1024]{1,2,0:T(8,128)(2,1)}, bf16[2,512,1024]{1,2,0:T(8,128)(2,1)}, u32[]{:S(2)}, u32[]{:S(2)}) collective-permute-start(bf16[2,512,1024]{1,2,0:T(8,128)(2,1)} %pad_maximum_fusion), channel_id=1, source_target_pairs={{0,4},{2,6},{4,8},{6,10},{8,12},{10,14},{12,16},{14,18},{16,20},{1... | collective-permute-start | bytes 6291464 | tf_op jit(solution)/shard_map/ppermute | solution.py:21
  19.4 1037.6 %reduce-scatter.2.cloned.1.call-start = ((), (), s32[]{:S(2)}) async-start(), calls=%async_computation.2 | async-start | bytes 4128768 | tf_op jit(solution)/shard_map/reduce_scatter | solution.py:89
  208.6 91.5 %copy-start.2 = (f32[8,128,128]{2,1,0:T(8,128)S(1)}, f32[8,128,128]{2,1,0:T(8,128)}, u32[]{:S(2)}) copy-start(f32[8,128,128]{2,1,0:T(8,128)} %all-reduce.2.cloned.1.call-done) | copy-start | bytes 1572868
  965.9 26.4 %copy-start.3 = (bf16[1,1536,1024]{1,2,0:T(8,128)(2,1)S(1)}, bf16[1,1536,1024]{1,2,0:T(8,128)(2,1)}, u32[]{:S(2)}) copy-start(bf16[1,1536,1024]{1,2,0:T(8,128)(2,1)} %get-tuple-element.11) | copy-start | bytes 9437188
  1044.2 1.6 copy-start.4
  1044.2 12.8 %copy-start.1 = (f32[8,128,64]{1,2,0:T(8,128)S(1)}, f32[8,128,64]{1,2,0:T(8,128)}, u32[]{:S(2)}) copy-start(f32[8,128,64]{1,2,0:T(8,128)} %param.11) | copy-start | bytes 786436
Sparse Core Ops, SparseCore 0:
  19.6 188.9 all-reduce.1
  1044.3 12.6 reduce-scatter.1
where the time goes:
time: 1070 us; the launch traced here: 1060 us
  other arithmetic  709 us (66%)
  waiting for transfers between devices  192 us (18%)
  matrix products  128 us (12%)
  between operations  15 us (1%)
  local copies, waits for them, and re-layouts  14.5 us (1%)
    another operation x25, other arithmetic, orthonormal(): factor_low = jnp.linalg.cholesky(inner_prod)  381 us
    another operation x17, other arithmetic, solve_one(): return jax.scipy.linalg.solve_triangular(factor, column.T, lower=True).T  316 us
    psum x1, waiting for transfers between devices, shards(): key_gram = lax.psum(local_gram, 'seq')  183 us
    sub x2, matrix products, attend(): raised = jnp.exp(scores - row_peak)  50 us
    dot_general x2, matrix products, attend(): jnp.einsum('hgts,shd->thgd', weights, value_rows, preferred_element_type=...  39.9 us
  transfers between devices with their start and end apart: 4, of which 2 were waited for; matrix products, arithmetic and copies ran while one was open for 69% of the time, Pallas kernels for 0%

commit v1 on v0

v1 whole, which is shorter than its diff:
```python
import functools
import math

import jax
import jax.numpy as jnp
from jax import lax
from jax.experimental import pallas as pl
from jax.experimental.pallas import tpu as pltpu
from jax.sharding import PartitionSpec as P

HQ = 32
HK = 16
HD = 128
QSCALE = 168
W = 1024
SWEEPS = 8
GROUP = HQ // HK
TILE = 128
PAIR = 2

HIGHEST = lax.Precision.HIGHEST
NEGLIGIBLE = -1e30
F32 = jnp.float32
BF16 = jnp.bfloat16


def from_behind(array, axis, by):
    peers = lax.axis_size(axis)
    pairs = [(i, i + by) for i in range(peers) if 0 <= i + by < peers]
    return lax.ppermute(array, axis, pairs)


def dot(a, b, dims, precision=None):
    return lax.dot_general(
        a, b, (dims, ((), ())), precision=precision, preferred_element_type=F32
    )


def gram_kernel(keys_ref, gram_ref):
    for head in range(gram_ref.shape[0]):
        block = keys_ref[:, head * HD:(head + 1) * HD]
        gram_ref[head] = dot(block, block, ((0,), (0,)))


def eliminate(work, heads, rank):
    for k in range(0, rank, PAIR):
        rows = [work[k + j] for j in range(PAIR)]
        corner = [[rows[j][:, k + m:k + m + 1] for m in range(PAIR)] for j in range(PAIR)]
        ratio = [[None] * PAIR for _ in range(PAIR)]
        scaled = []
        for j in range(PAIR):
            inverse = 1.0 / corner[j][j]
            scaled.append(rows[j] * inverse)
            for m in range(j + 1, PAIR):
                ratio[j][m] = corner[j][m] * inverse
            for l in range(j + 1, PAIR):
                rows[l] = rows[l] - corner[l][j] * scaled[j]
                for m in range(j + 1, PAIR):
                    corner[l][m] = corner[l][m] - corner[l][j] * ratio[j][m]
        for j in range(PAIR):
            work[k + j] = rows[j] * lax.rsqrt(corner[j][j])
        if k + PAIR < rank:
            rest = work[k + PAIR:]
            factors = [rest[:, :, k + m:k + m + 1] for m in range(PAIR)]
            for j in range(PAIR):
                for m in range(j + 1, PAIR):
                    factors[m] = factors[m] - factors[j] * ratio[j][m][None]
                rest = rest - factors[j] * scaled[j][None]
            work[k + PAIR:] = rest


def basis_kernel(gram_ref, start_ref, half_ref, basis, product, work):
    heads, _, rank = start_ref.shape
    basis[...] = start_ref[...]
    lane = lax.broadcasted_iota(jnp.int32, (rank, rank), 1)
    unit = jnp.where(lax.broadcasted_iota(jnp.int32, (rank, rank), 0) == lane, 1.0, 0.0)

    def sweep(_, carry):
        for head in range(heads):
            z = dot(gram_ref[head], basis[head], ((1,), (0,)), HIGHEST)
            product[head] = z
            inner = dot(z, z, ((0,), (0,)), HIGHEST)
            work[:, head, :] = jnp.concatenate([inner, unit], axis=1)
        eliminate(work, heads, rank)
        for head in range(heads):
            inverse = work[:, head, :][:, rank:]
            basis[head] = dot(product[head], inverse, ((1,), (1,)), HIGHEST)
        return carry

    lax.fori_loop(0, SWEEPS, sweep, 0)
    half_ref[...] = basis[...].astype(BF16)


def soft(queries, keys, values, low_mask, high_mask):
    scores = dot(queries, keys, ((1,), (1,)))
    scores = jnp.concatenate(
        [
            jnp.where(low_mask, scores[:, :TILE], NEGLIGIBLE),
            scores[:, TILE:-TILE],
            jnp.where(high_mask, scores[:, -TILE:], NEGLIGIBLE),
        ],
        axis=1,
    )
    peak = jnp.max(scores, axis=-1, keepdims=True)
    raised = jnp.exp2((scores - peak) * (QSCALE ** (-0.5) * math.log2(math.e)))
    both = dot(raised.astype(BF16), values, ((1,), (0,)))
    return both[:, :HD] / both[:, HD:]


def attend_kernel(prior, *refs):
    query_ref = refs[0]
    key_refs = refs[1:prior + 2]
    value_refs = refs[prior + 2:2 * prior + 3]
    half_ref, low_ref, gap_ref, window_k, window_v, window_low = refs[2 * prior + 3:]
    rows = query_ref.shape[0]
    where_at = lax.axis_index("seq")
    first = key_refs[prior][0:1, :]
    for distance in range(1, prior + 1):
        first = jnp.where(where_at >= distance, key_refs[prior - distance][0:1, :], first)
    for block in range(prior + 1):
        real = where_at >= prior - block
        part = pl.ds(block * rows, rows)
        window_k[part, :] = jnp.where(real, key_refs[block][...], first)
        window_v[part, :HD] = value_refs[block][...]
        window_v[part, HD:] = jnp.where(
            real, jnp.ones((rows, HD), BF16), jnp.zeros((rows, HD), BF16)
        )
    half = half_ref[0]
    window_low[...] = dot(window_k[...], half, ((1,), (0,))).astype(BF16)
    row = lax.broadcasted_iota(jnp.int32, (TILE, TILE), 0)
    column = lax.broadcasted_iota(jnp.int32, (TILE, TILE), 1)
    low_mask = jnp.concatenate([column > row] * GROUP, axis=0)
    high_mask = jnp.concatenate([column <= row] * GROUP, axis=0)
    for start in range(0, rows, TILE):
        queries = jnp.concatenate(
            [query_ref[start:start + TILE, g * HD:(g + 1) * HD] for g in range(GROUP)], axis=0
        )
        low_queries = dot(queries, half, ((1,), (0,))).astype(BF16)
        part = pl.ds(start, W + TILE)
        values = window_v[part, :]
        exact = soft(queries, window_k[part, :], values, low_mask, high_mask)
        approx = soft(low_queries, window_low[part, :], values, low_mask, high_mask)
        gap = (exact - approx).astype(BF16)
        approx = approx.astype(BF16)
        for g in range(GROUP):
            low_ref[start:start + TILE, g * HD:(g + 1) * HD] = approx[g * TILE:(g + 1) * TILE]
            gap_ref[start:start + TILE, g * HD:(g + 1) * HD] = gap[g * TILE:(g + 1) * TILE]


def shards(queries, keys, values, start_basis, out_weight):
    tok_rows = keys.shape[0]
    heads, _, rank = start_basis.shape
    prior = W // tok_rows
    local_gram = pl.pallas_call(
        gram_kernel,
        out_shape=jax.ShapeDtypeStruct((heads, HD, HD), F32),
        compiler_params=pltpu.CompilerParams(vmem_limit_bytes=24 << 20),
        cost_estimate=pl.CostEstimate(
            flops=2 * tok_rows * HD * HD * heads, bytes_accessed=2 << 20, transcendentals=0
        ),
        name="gram",
    )(keys)
    key_gram = lax.psum(local_gram, "seq")
    key_blocks = [from_behind(keys, "seq", d) for d in range(prior, 0, -1)] + [keys]
    value_blocks = [from_behind(values, "seq", d) for d in range(prior, 0, -1)] + [values]
    basis_half = pl.pallas_call(
        basis_kernel,
        out_shape=jax.ShapeDtypeStruct((heads, HD, rank), BF16),
        scratch_shapes=[
            pltpu.VMEM((heads, HD, rank), F32),
            pltpu.VMEM((heads, HD, rank), F32),
            pltpu.VMEM((rank, heads, 2 * rank), F32),
        ],
        compiler_params=pltpu.CompilerParams(vmem_limit_bytes=24 << 20),
        cost_estimate=pl.CostEstimate(
            flops=40_000_000_000, bytes_accessed=2 << 20, transcendentals=0
        ),
        name="basis",
    )(key_gram, start_basis)

    wide = pl.BlockSpec((tok_rows, GROUP * HD), lambda h: (0, h))
    narrow = pl.BlockSpec((tok_rows, HD), lambda h: (0, h))
    span = (prior + 1) * tok_rows
    lowrank_attn, gap = pl.pallas_call(
        functools.partial(attend_kernel, prior),
        grid=(heads,),
        in_specs=[wide]
        + [narrow] * (2 * prior + 2)
        + [pl.BlockSpec((1, HD, rank), lambda h: (h, 0, 0))],
        out_specs=[wide, wide],
        out_shape=[jax.ShapeDtypeStruct(queries.shape, BF16)] * 2,
        scratch_shapes=[
            pltpu.VMEM((span, HD), BF16),
            pltpu.VMEM((span, 2 * HD), BF16),
            pltpu.VMEM((span, rank), BF16),
        ],
        compiler_params=pltpu.CompilerParams(vmem_limit_bytes=48 << 20),
        cost_estimate=pl.CostEstimate(
            flops=30_000_000_000, bytes_accessed=16 << 20, transcendentals=40_000_000
        ),
        name="attend",
    )(queries, *key_blocks, *value_blocks, basis_half)

    peers = lax.axis_size("head")
    if peers == 2:
        mine = lax.axis_index("head")
        half_rows = tok_rows // 2

        def project(which):
            rows = lax.dynamic_slice_in_dim(gap, which * half_rows, half_rows, 0)
            return jnp.dot(rows, out_weight, preferred_element_type=F32).astype(BF16)

        arrived = lax.ppermute(project(1 - mine), "head", [(0, 1), (1, 0)])
        deviation = (project(mine).astype(F32) + arrived.astype(F32)).astype(BF16)
    else:
        deviation = lax.psum_scatter(
            jnp.dot(gap, out_weight, preferred_element_type=F32).astype(BF16),
            "head",
            scatter_dimension=0,
            tiled=True,
        )
    return (lowrank_attn, deviation)


def solution(mesh):
    placed = (
        P("seq", "head"),
        P("seq", "head"),
        P("seq", "head"),
        P("head", None, None),
        P("head", None),
    )
    return jax.shard_map(
        shards,
        mesh=mesh,
        in_specs=placed,
        out_specs=(P("seq", "head"), P(("seq", "head"), None)),
        check_vma=False,
    )
```

time: 1070 us -> 343 us (0.32)
  other arithmetic: 709 us -> 0 us
  Pallas kernels: 0 us -> 145 us
  matrix products: 128 us -> 17.4 us
  waiting for transfers between devices: 192 us -> 146 us
  local copies, waits for them, and re-layouts: 14.5 us -> 2.47 us
    another operation x43 -> x0, other arithmetic: 699 us -> none  [the longest x25 381 us: orthonormal(): factor_low = jnp.linalg.cholesky(inner_prod)]
    pallas_call x0 -> x3, Pallas kernels: none -> 145 us  [the longest x1 106 us: shards(): pl.pallas_call(basis_kernel, out_shape=jax.ShapeDtypeStruct((heads, HD, r...]
    dot_general x22 -> x2, matrix products: 72.9 us -> 17.4 us  [project(): return jnp.dot(rows, out_weight, preferred_element_type=F32).astype(BF16)]
    sub x2 -> x0, matrix products: 50 us -> none  [attend(): raised = jnp.exp(scores - row_peak)]
    psum x1, waiting for transfers between devices: 183 us -> 143 us  [shards(): key_gram = lax.psum(local_gram, 'seq')]
  transfers between devices with their start and end apart: 4 -> 6, of which waited for: 2 -> 2; matrix products, arithmetic and copies ran while one was open for 69% -> 0% of each run, Pallas kernels for 0% -> 31%
where the time goes in v1:
time: 343 us; the launch traced here: 341 us
  waiting for transfers between devices  146 us (43%)
  Pallas kernels  145 us (42%)
  matrix products  17.4 us (5%)
  starting transfers between devices  15.1 us (4%)
  between operations  14.1 us (4%)
    psum x1, waiting for transfers between devices, shards(): key_gram = lax.psum(local_gram, 'seq')  143 us
    pallas_call x1, Pallas kernels, shards(): pl.pallas_call(basis_kernel, out_shape=jax.ShapeDtypeStruct((heads, HD, r...  106 us
    pallas_call x1, Pallas kernels, shards(): pl.pallas_call(functools.partial(attend_kernel, prior), grid=(heads,), in...  37.9 us
    dot_general x2, matrix products, project(): return jnp.dot(rows, out_weight, preferred_element_type=F32).astype(BF16)  17.4 us
    ppermute x4, starting transfers between devices, from_behind(): return lax.ppermute(array, axis, pairs)  12.5 us
  transfers between devices with their start and end apart: 6, of which 2 were waited for; matrix products, arithmetic and copies ran while one was open for 0% of the time, Pallas kernels for 31%

profile of v1, /device:TPU:13, one launch (start us, length us, event | category | flops | bytes accessed | tf_op | source)
XLA Modules:
  0.0 340.6 jit_solution(1157061573710361892)
XLA Ops:
  7.2 0.0 all-reduce.2.cloned.1.call-start
  7.2 0.0 copy-start
  7.2 1.2 copy-done
  8.4 0.0 copy-start.1
  8.4 0.0 copy-start.3
  8.4 1.3 gram.1
  9.7 0.0 all-reduce.2.cloned.1.call-update
  9.8 0.0 copy-done.1
  9.8 3.1 collective-permute-start
  12.9 3.1 collective-permute-start.1
  16.0 3.2 collective-permute-start.2
  19.2 3.1 collective-permute-start.3
  22.3 0.0 copy-done.3
  22.3 0.2 copy.7.start_ref
  22.6 143.1 %all-reduce.2.cloned.1.call-done.gram_ref = f32[8,128,128]{2,1,0:T(8,128)} async-done(((f32[8,128,128]{2,1,0:T(8,128)}), f32[8,128,128]{2,1,0:T(8,128)}) %all-reduce.2.cloned.1.call-update) | async-done | bytes 524304 | tf_op jit(solution)/shard_map/psum | solution.py:163
  165.7 0.0 copy-start.2
  165.7 1.0 copy-done.2
  166.7 106.3 %basis.1.refs_7_ = bf16[8,128,64]{2,1,0:T(8,128)(2,1)S(1)} custom-call(f32[8,128,128]{2,1,0:T(8,128)S(1)} %copy-done.2, f32[8,128,64]{2,1,0:T(8,128)S(1)} %copy.7.start_ref), custom_call_target="tpu_custom_call" | custom-call | flops 40000000000 | bytes 2097152 | tf_op jit(solution)/shard_map/basis/pallas_call | solution.py:166
  273.0 0.0 collective-permute-done.refs_1_
  273.0 0.0 collective-permute-done.1.refs_2_
  273.0 0.0 collective-permute-done.2.refs_4_
  273.1 0.0 collective-permute-done.3.refs_5_
  273.1 37.9 %attend.1 = (bf16[512,2048]{1,0:T(8,128)(2,1)}, bf16[512,2048]{1,0:T(8,128)(2,1)}) custom-call(bf16[512,2048]{1,0:T(8,128)(2,1)} %refs_0_.1, bf16[512,1024]{1,0:T(8,128)(2,1)S(1)} %collective-permute-done.refs_1_, bf16[512,1024]{1,0:T(8,128)(2,1)} %collective-permute-done.1.refs_2_, bf16[512,1024]{1,0:T(8,128)(2,1)S(1)} %copy-done.1, ...), custom_call_target="tpu_custom_call" | custom-call | flops 30000001024 | bytes 16777216 | tf_op jit(solution)/shard_map/attend/pallas_call | solution.py:184
  310.9 8.7 %convolution_convert_fusion = bf16[256,2688]{1,0:T(8,128)(2,1)} fusion(bf16[2048,2688]{1,0:T(8,128)(2,1)} %param.9, bf16[512,2048]{1,0:T(8,128)(2,1)} %get-tuple-element.5, s32[]{:T(128)S(6)} %select_n.7), kind=kOutput, calls=%fused_computation | convolution fusion | flops 2819260416 | bytes 13434884 | tf_op jit(solution)/shard_map/dot_general | solution.py:211
  319.6 2.5 collective-permute-start.4
  322.1 3.0 collective-permute-done.4
  325.1 8.7 %fusion.2 = bf16[256,2688]{1,0:T(8,128)(2,1)} fusion(bf16[2048,2688]{1,0:T(8,128)(2,1)} %param.9, bf16[256,2688]{1,0:T(8,128)(2,1)S(1)} %collective-permute-done.4, bf16[512,2048]{1,0:T(8,128)(2,1)} %get-tuple-element.5, s32[]{:T(128)S(6)} %select_n.6), kind=kOutput, calls=%fused_computation.4 | convolution fusion | flops 2822012928 | bytes 14811140 | tf_op jit(solution)/shard_map/dot_general | solution.py:211
Async XLA Ops:
  7.2 158.5 %all-reduce.2.cloned.1.call-start = ((), (), s32[]{:S(2)}) async-start(), calls=%async_computation | async-start | bytes 1048576 | tf_op jit(solution)/shard_map/psum | solution.py:163
  7.2 1.2 copy-start
  8.4 1.3 copy-start.1
  8.4 13.9 %copy-start.3 = (f32[8,128,64]{1,2,0:T(8,128)S(1)}, f32[8,128,64]{1,2,0:T(8,128)}, u32[]{:S(2)}) copy-start(f32[8,128,64]{1,2,0:T(8,128)} %param.8) | copy-start | bytes 786436
  9.8 263.3 %collective-permute-start = (bf16[512,1024]{1,0:T(8,128)(2,1)S(1)}, bf16[512,1024]{1,0:T(8,128)(2,1)S(1)}, u32[]{:S(2)}, u32[]{:S(2)}) collective-permute-start(bf16[512,1024]{1,0:T(8,128)(2,1)S(1)} %copy-done.1), channel_id=1, source_target_pairs={{0,4},{2,6},{4,8},{6,10},{8,12},{10,14},{12,16},{14,18},{16,20},{1... | collective-permute-start | bytes 3145736 | tf_op jit(solution)/shard_map/ppermute | solution.py:30
  12.9 260.1 %collective-permute-start.1 = (bf16[512,1024]{1,0:T(8,128)(2,1)S(1)}, bf16[512,1024]{1,0:T(8,128)(2,1)}, u32[]{:S(2)}, u32[]{:S(2)}) collective-permute-start(bf16[512,1024]{1,0:T(8,128)(2,1)S(1)} %copy-done.1), channel_id=1, source_target_pairs={{0,2},{2,4},{4,6},{6,8},{8,10},{10,12},{12,14},{14,16},{16,18},{18... | collective-permute-start | bytes 3145736 | tf_op jit(solution)/shard_map/ppermute | solution.py:30
  16.0 257.0 %collective-permute-start.2 = (bf16[512,1024]{1,0:T(8,128)(2,1)}, bf16[512,1024]{1,0:T(8,128)(2,1)}, u32[]{:S(2)}, u32[]{:S(2)}) collective-permute-start(bf16[512,1024]{1,0:T(8,128)(2,1)} %refs_6_.1), channel_id=1, source_target_pairs={{0,4},{2,6},{4,8},{6,10},{8,12},{10,14},{12,16},{14,18},{16,20},{1... | collective-permute-start | bytes 3145736 | tf_op jit(solution)/shard_map/ppermute | solution.py:30
  19.2 253.8 %collective-permute-start.3 = (bf16[512,1024]{1,0:T(8,128)(2,1)}, bf16[512,1024]{1,0:T(8,128)(2,1)}, u32[]{:S(2)}, u32[]{:S(2)}) collective-permute-start(bf16[512,1024]{1,0:T(8,128)(2,1)} %refs_6_.1), channel_id=1, source_target_pairs={{0,2},{2,4},{4,6},{6,8},{8,10},{10,12},{12,14},{14,16},{16,18},{18... | collective-permute-start | bytes 3145736 | tf_op jit(solution)/shard_map/ppermute | solution.py:30
  165.7 1.0 copy-start.2
  319.6 5.5 %collective-permute-start.4 = (bf16[256,2688]{1,0:T(8,128)(2,1)}, bf16[256,2688]{1,0:T(8,128)(2,1)S(1)}, u32[]{:S(2)}, u32[]{:S(2)}) collective-permute-start(bf16[256,2688]{1,0:T(8,128)(2,1)} %convolution_convert_fusion), channel_id=1, source_target_pairs={{0,1},{1,0},{2,3},{3,2},{4,5},{5,4},{6,7},{7,6},{8,9},{9,8},{10,11... | collective-permute-start | bytes 4128776 | tf_op jit(solution)/shard_map/ppermute | solution.py:213
Sparse Core Ops, SparseCore 0:
  13.7 151.9 all-reduce.1

commit v2 on v1

--- a/solution.py
+++ b/solution.py
@@ -16,7 +16,8 @@
 SWEEPS = 8
 GROUP = HQ // HK
 TILE = 128
-PAIR = 2
+STEP = 4
+SUB = 8
 
 HIGHEST = lax.Precision.HIGHEST
 NEGLIGIBLE = -1e30
@@ -42,53 +43,94 @@
         gram_ref[head] = dot(block, block, ((0,), (0,)))
 
 
-def eliminate(work, heads, rank):
-    for k in range(0, rank, PAIR):
-        rows = [work[k + j] for j in range(PAIR)]
-        corner = [[rows[j][:, k + m:k + m + 1] for m in range(PAIR)] for j in range(PAIR)]
-        ratio = [[None] * PAIR for _ in range(PAIR)]
+def inverse_factor(inner, unit):
+    rank = inner.shape[0]
+    whole = jnp.concatenate([inner, unit], axis=1)
+    width = whole.shape[1]
+    blocks = [whole[at:at + SUB] for at in range(0, rank, SUB)]
+    level = lax.broadcasted_iota(jnp.int32, (SUB, width), 0)
+    for k in range(0, rank, STEP):
+        own, inside = k // SUB, k % SUB
+        rows = [
+            jnp.broadcast_to(blocks[own][inside + j:inside + j + 1], (SUB, width))
+            for j in range(STEP)
+        ]
+        corner = [
+            [
+                jnp.broadcast_to(rows[j][:, k + m:k + m + 1], (SUB, width))
+                for m in range(STEP)
+            ]
+            for j in range(STEP)
+        ]
+        ratio = [[None] * STEP for _ in range(STEP)]
         scaled = []
-        for j in range(PAIR):
+        for j in range(STEP):
             inverse = 1.0 / corner[j][j]
             scaled.append(rows[j] * inverse)
-            for m in range(j + 1, PAIR):
+            for m in range(j + 1, STEP):
                 ratio[j][m] = corner[j][m] * inverse
-            for l in range(j + 1, PAIR):
+            for l in range(j + 1, STEP):
                 rows[l] = rows[l] - corner[l][j] * scaled[j]
-                for m in range(j + 1, PAIR):
+                for m in range(j + 1, STEP):
                     corner[l][m] = corner[l][m] - corner[l][j] * ratio[j][m]
-        for j in range(PAIR):
-            work[k + j] = rows[j] * lax.rsqrt(corner[j][j])
-        if k + PAIR < rank:
-            rest = work[k + PAIR:]
-            factors = [rest[:, :, k + m:k + m + 1] for m in range(PAIR)]
-            for j in range(PAIR):
-                for m in range(j + 1, PAIR):
-                    factors[m] = factors[m] - factors[j] * ratio[j][m][None]
-                rest = rest - factors[j] * scaled[j][None]
-            work[k + PAIR:] = rest
-
-
-def basis_kernel(gram_ref, start_ref, half_ref, basis, product, work):
-    heads, _, rank = start_ref.shape
-    basis[...] = start_ref[...]
+        for at in range(own, len(blocks)):
+            block = blocks[at]
+            if at > own or inside + STEP < SUB:
+                factors = [
+                    jnp.broadcast_to(block[:, k + m:k + m + 1], (SUB, width))
+                    for m in range(STEP)
+                ]
+                for j in range(STEP):
+                    for m in range(j + 1, STEP):
+                        factors[m] = factors[m] - factors[j] * ratio[j][m]
+                    block = block - factors[j] * scaled[j]
+            if at == own:
+                block = jnp.where(level < inside, blocks[own], block)
+                for j in range(STEP):
+                    done = rows[j] * lax.rsqrt(corner[j][j])
+                    block = jnp.where(level == inside + j, done, block)
+            blocks[at] = block
+    return jnp.concatenate(blocks, axis=0)[:, rank:]
+
+
+def basis_kernel(gram_ref, start_ref, half_ref, basis):
+    rank = start_ref.shape[2]
+    basis[...] = start_ref[0]
     lane = lax.broadcasted_iota(jnp.int32, (rank, rank), 1)
     unit = jnp.where(lax.broadcasted_iota(jnp.int32, (rank, rank), 0) == lane, 1.0, 0.0)
 
     def sweep(_, carry):
-        for head in range(heads):
-            z = dot(gram_ref[head], basis[head], ((1,), (0,)), HIGHEST)
-            product[head] = z
-            inner = dot(z, z, ((0,), (0,)), HIGHEST)
-            work[:, head, :] = jnp.concatenate([inner, unit], axis=1)
-        eliminate(work, heads, rank)
-        for head in range(heads):
-            inverse = work[:, head, :][:, rank:]
-            basis[head] = dot(product[head], inverse, ((1,), (1,)), HIGHEST)
+        z = dot(gram_ref[0], basis[...], ((1,), (0,)), HIGHEST)
+        inner = dot(z, z, ((0,), (0,)), HIGHEST)
+        basis[...] = dot(z, inverse_factor(inner, unit), ((1,), (1,)), HIGHEST)
         return carry
 
     lax.fori_loop(0, SWEEPS, sweep, 0)
-    half_ref[...] = basis[...].astype(BF16)
+    half_ref[0] = basis[...].astype(BF16)
+
+
+def subspace(gram, start):
+    heads, _, rank = start.shape
+    return pl.pallas_call(
+        basis_kernel,
+        grid=(heads,),
+        in_specs=[
+            pl.BlockSpec((1, HD, HD), lambda h: (h, 0, 0)),
+            pl.BlockSpec((1, HD, rank), lambda h: (h, 0, 0)),
+        ],
+        out_specs=pl.BlockSpec((1, HD, rank), lambda h: (h, 0, 0)),
+        out_shape=jax.ShapeDtypeStruct((heads, HD, rank), BF16),
+        scratch_shapes=[pltpu.VMEM((HD, rank), F32)],
+        compiler_params=pltpu.CompilerParams(vmem_limit_bytes=24 << 20),
+        cost_estimate=pl.CostEstimate(
+            flops=40_000_000_000, bytes_accessed=2 << 20, transcendentals=0
+        ),
+        name="basis",
+    )(gram, start)
+
+
+def partner(array, axis, mask):
+    return lax.ppermute(array, axis, [(i, i ^ mask) for i in range(lax.axis_size(axis))])
 
 
 def soft(queries, keys, values, low_mask, high_mask):
@@ -160,23 +202,42 @@
         ),
         name="gram",
     )(keys)
-    key_gram = lax.psum(local_gram, "seq")
+    peers = lax.axis_size("seq")
+    where_at = lax.axis_index("seq")
+    spread = peers >= heads and peers & (peers - 1) == 0 and heads & (heads - 1) == 0
+    if spread:
+        total, left, bit = local_gram, heads, 1
+        while bit < peers:
+            if left > 1:
+                left //= 2
+                upper = (where_at & bit) != 0
+                sent = jnp.where(upper, total[:left], total[left:])
+                total = jnp.where(upper, total[left:], total[:left]) + partner(sent, "seq", bit)
+            else:
+                total = total + partner(total, "seq", bit)
+            bit *= 2
+        total, keys, values = lax.optimization_barrier((total, keys, values))
+    else:
+        total = lax.psum(local_gram, "seq")
     key_blocks = [from_behind(keys, "seq", d) for d in range(prior, 0, -1)] + [keys]
     value_blocks = [from_behind(values, "seq", d) for d in range(prior, 0, -1)] + [values]
-    basis_half = pl.pallas_call(
-        basis_kernel,
-        out_shape=jax.ShapeDtypeStruct((heads, HD, rank), BF16),
-        scratch_shapes=[
-            pltpu.VMEM((heads, HD, rank), F32),
-            pltpu.VMEM((heads, HD, rank), F32),
-            pltpu.VMEM((rank, heads, 2 * rank), F32),
-        ],
-        compiler_params=pltpu.CompilerParams(vmem_limit_bytes=24 << 20),
-        cost_estimate=pl.CostEstimate(
-            flops=40_000_000_000, bytes_accessed=2 << 20, transcendentals=0
-        ),
-        name="basis",
-    )(key_gram, start_basis)
+    if spread:
+        owner, left, bit = 0, heads, 1
+        while left > 1:
+            left //= 2
+            owner = owner + jnp.where((where_at & bit) != 0, left, 0)
+            bit *= 2
+        start = lax.dynamic_slice_in_dim(start_basis, owner, 1, 0)
+        basis_half = subspace(total, start)
+        while bit > 1:
+            bit //= 2
+            upper = (where_at & bit) != 0
+            other = partner(basis_half, "seq", bit)
+            basis_half = jnp.concatenate(
+                [jnp.where(upper, other, basis_half), jnp.where(upper, basis_half, other)], axis=0
+            )
+    else:
+        basis_half = subspace(total, start_basis)
 
     wide = pl.BlockSpec((tok_rows, GROUP * HD), lambda h: (0, h))
     narrow = pl.BlockSpec((tok_rows, HD), lambda h: (0, h))

time: 343 us -> 216 us (0.63)
  Pallas kernels: 145 us -> 66.8 us
  waiting for transfers between devices: 146 us -> 110 us
  between operations: 14.1 us -> 0.85 us
  starting transfers between devices: 15.1 us -> 19 us
    psum x1 -> x0, waiting for transfers between devices: 143 us -> none  [shards(): key_gram = lax.psum(local_gram, 'seq')]
    ppermute x0 -> x7, waiting for transfers between devices: none -> 107 us  [partner(): lax.ppermute(array, axis, [(i, i ^ mask) for i in range(lax.axis_size(axi...]
    pallas_call x1, Pallas kernels: 106 us -> 28.1 us  [subspace(): pl.pallas_call(basis_kernel, grid=(heads,), in_specs=[pl.BlockSpec((1, HD...]
    ppermute x0 -> x7, starting transfers between devices: none -> 5.75 us  [partner(): lax.ppermute(array, axis, [(i, i ^ mask) for i in range(lax.axis_size(axi...]
  transfers between devices with their start and end apart: 6 -> 12, of which waited for: 2 -> 7; matrix products, arithmetic and copies ran while one was open for 0% -> 1% of each run, Pallas kernels for 31% -> 0%
where the time goes in v2:
time: 216 us
  waiting for transfers between devices  110 us (51%)
  Pallas kernels  66.8 us (31%)
  starting transfers between devices  19 us (9%)
  matrix products  16.3 us (8%)
    ppermute x7, waiting for transfers between devices, partner(): lax.ppermute(array, axis, [(i, i ^ mask) for i in range(lax.axis_size(axi...  107 us
    pallas_call x1, Pallas kernels, shards(): pl.pallas_call(functools.partial(attend_kernel, prior), grid=(heads,), in...  38.1 us
    pallas_call x1, Pallas kernels, subspace(): pl.pallas_call(basis_kernel, grid=(heads,), in_specs=[pl.BlockSpec((1, HD...  28.1 us
    dot_general x2, matrix products, project(): return jnp.dot(rows, out_weight, preferred_element_type=F32).astype(BF16)  16.3 us
    ppermute x4, starting transfers between devices, from_behind(): return lax.ppermute(array, axis, pairs)  12.7 us
    ppermute x7, starting transfers between devices, partner(): lax.ppermute(array, axis, [(i, i ^ mask) for i in range(lax.axis_size(axi...  5.75 us
  transfers between devices with their start and end apart: 12, of which 7 were waited for; matrix products, arithmetic and copies ran while one was open for 1% of the time, Pallas kernels for 0%

profile of v2, /device:TPU:13, one launch (start us, length us, event | category | flops | bytes accessed | tf_op | source)
XLA Modules:
  0.0 216.2 jit_solution(2736401590330894605)
XLA Ops:
  0.6 0.0 copy-start
  0.7 0.0 copy-start.1
  0.7 1.3 copy-done.1
  1.9 0.5 gram.1
  2.5 1.3 collective-permute-start
  3.7 6.0 %collective-permute-done = f32[4,128,128]{2,1,0:T(8,128)S(1)} collective-permute-done((f32[4,128,128]{2,1,0:T(8,128)S(1)}, f32[4,128,128]{2,1,0:T(8,128)S(1)}, u32[]{:S(2)}, u32[]{:S(2)}) %collective-permute-start) | collective-permute-done | bytes 262176 | tf_op jit(solution)/shard_map/ppermute | solution.py:133
  9.8 0.3 collective-permute-start.1
  10.1 3.6 %collective-permute-done.1 = f32[2,128,128]{2,1,0:T(8,128)S(1)} collective-permute-done((f32[2,128,128]{2,1,0:T(8,128)S(1)}, f32[2,128,128]{2,1,0:T(8,128)S(1)}, u32[]{:S(2)}, u32[]{:S(2)}) %collective-permute-start.1) | collective-permute-done | bytes 131104 | tf_op jit(solution)/shard_map/ppermute | solution.py:133
  13.7 0.2 collective-permute-start.2
  13.9 3.0 %collective-permute-done.2 = f32[1,128,128]{2,1,0:T(8,128)S(1)} collective-permute-done((f32[1,128,128]{2,1,0:T(8,128)S(1)}, f32[1,128,128]{2,1,0:T(8,128)S(1)}, u32[]{:S(2)}, u32[]{:S(2)}) %collective-permute-start.2) | collective-permute-done | bytes 65568 | tf_op jit(solution)/shard_map/ppermute | solution.py:133
  16.9 2.4 %collective-permute-start.3 = (f32[1,128,128]{2,1,0:T(8,128)S(1)}, f32[1,128,128]{2,1,0:T(8,128)S(1)}, u32[]{:S(2)}, u32[]{:S(2)}) collective-permute-start(f32[1,128,128]{2,1,0:T(8,128)S(1)} %select_add_fusion.2), channel_id=1, source_target_pairs={{0,16},{2,18},{4,20},{6,22},{8,24},{10,26},{12,28},{14,30},{16,0},... | collective-permute-start | bytes 196616 | tf_op jit(solution)/shard_map/ppermute | solution.py:133
  19.3 0.0 copy-done
  19.3 0.1 copy.8.start_ref
  19.4 2.2 %collective-permute-done.3 = f32[1,128,128]{2,1,0:T(8,128)S(1)} collective-permute-done((f32[1,128,128]{2,1,0:T(8,128)S(1)}, f32[1,128,128]{2,1,0:T(8,128)S(1)}, u32[]{:S(2)}, u32[]{:S(2)}) %collective-permute-start.3) | collective-permute-done | bytes 65568 | tf_op jit(solution)/shard_map/ppermute | solution.py:133
  21.6 0.0 copy-start.2
  21.6 28.1 %basis.1 = bf16[1,128,64]{2,1,0:T(8,128)(2,1)S(1)} custom-call(f32[1,128,128]{2,1,0:T(8,128)S(1)} %add.33.gram_ref, f32[1,128,64]{2,1,0:T(8,128)S(1)} %copy.8.start_ref), custom_call_target="tpu_custom_call" | custom-call | flops 40000000000 | bytes 2097152 | tf_op jit(solution)/shard_map/basis/pallas_call | solution.py:114
  49.8 0.1 collective-permute-start.8
  49.8 0.0 copy-done.2
  49.9 4.4 %collective-permute-start.4 = (bf16[512,1024]{1,0:T(8,128)(2,1)S(1)}, bf16[512,1024]{1,0:T(8,128)(2,1)S(1)}, u32[]{:S(2)}, u32[]{:S(2)}) collective-permute-start(bf16[512,1024]{1,0:T(8,128)(2,1)S(1)} %copy-done.2), channel_id=1, source_target_pairs={{0,4},{2,6},{4,8},{6,10},{8,12},{10,14},{12,16},{14,18},{16,20},{1... | collective-permute-start | bytes 3145736 | tf_op jit(solution)/shard_map/ppermute | solution.py:31
  54.2 3.1 %collective-permute-start.5 = (bf16[512,1024]{1,0:T(8,128)(2,1)S(1)}, bf16[512,1024]{1,0:T(8,128)(2,1)S(1)}, u32[]{:S(2)}, u32[]{:S(2)}) collective-permute-start(bf16[512,1024]{1,0:T(8,128)(2,1)S(1)} %copy-done.2), channel_id=1, source_target_pairs={{0,2},{2,4},{4,6},{6,8},{8,10},{10,12},{12,14},{14,16},{16,18},{18... | collective-permute-start | bytes 3145736 | tf_op jit(solution)/shard_map/ppermute | solution.py:31
  57.4 3.1 %collective-permute-start.6 = (bf16[512,1024]{1,0:T(8,128)(2,1)}, bf16[512,1024]{1,0:T(8,128)(2,1)}, u32[]{:S(2)}, u32[]{:S(2)}) collective-permute-start(bf16[512,1024]{1,0:T(8,128)(2,1)} %refs_6_), channel_id=1, source_target_pairs={{0,4},{2,6},{4,8},{6,10},{8,12},{10,14},{12,16},{14,18},{16,20},{1... | collective-permute-start | bytes 3145736 | tf_op jit(solution)/shard_map/ppermute | solution.py:31
  60.5 2.1 collective-permute-start.7
  62.6 0.0 collective-permute-done.8
  62.7 1.5 collective-permute-start.9
  64.2 76.2 %collective-permute-done.9 = bf16[2,128,64]{2,1,0:T(8,128)(2,1)S(1)} collective-permute-done((bf16[2,128,64]{2,1,0:T(8,128)(2,1)S(1)}, bf16[2,128,64]{2,1,0:T(8,128)(2,1)S(1)}, u32[]{:S(2)}, u32[]{:S(2)}) %collective-permute-start.9) | collective-permute-done | bytes 32800 | tf_op jit(solution)/shard_map/ppermute | solution.py:133
  140.4 0.7 pad_maximum_fusion.1
  141.1 0.0 collective-permute-start.10
  141.1 16.3 %collective-permute-done.10 = bf16[4,128,64]{2,1,0:T(8,128)(2,1)} collective-permute-done((bf16[4,128,64]{2,1,0:T(8,128)(2,1)}, bf16[4,128,64]{2,1,0:T(8,128)(2,1)}, u32[]{:S(2)}, u32[]{:S(2)}) %collective-permute-start.10) | collective-permute-done | bytes 65568 | tf_op jit(solution)/shard_map/ppermute | solution.py:133
  157.4 0.9 broadcast_select_fusion.1
  158.4 0.1 pad_maximum_fusion.refs_7_
  158.4 0.0 collective-permute-done.4.refs_1_
  158.4 0.0 collective-permute-done.5.refs_2_
  158.4 0.0 collective-permute-done.6.refs_4_
  158.5 0.0 collective-permute-done.7.refs_5_
  158.5 38.1 %attend.1 = (bf16[512,2048]{1,0:T(8,128)(2,1)}, bf16[512,2048]{1,0:T(8,128)(2,1)}) custom-call(bf16[512,2048]{1,0:T(8,128)(2,1)} %refs_0_.1, bf16[512,1024]{1,0:T(8,128)(2,1)S(1)} %collective-permute-done.4.refs_1_, bf16[512,1024]{1,0:T(8,128)(2,1)S(1)} %collective-permute-done.5.refs_2_, bf16[512,1024]{1,0:T(8,128)(2,1)S(1)} %copy-done.2, ...), custom_call_target="tpu_custom_call" | custom-call | flops 30000001024 | bytes 16777216 | tf_op jit(solution)/shard_map/attend/pallas_call | solution.py:245
  196.6 7.6 %convolution_convert_fusion = bf16[256,2688]{1,0:T(8,128)(2,1)S(1)} fusion(bf16[2048,2688]{1,0:T(8,128)(2,1)} %param.9, bf16[512,2048]{1,0:T(8,128)(2,1)} %get-tuple-element.11, s32[]{:T(128)S(6)} %select_n.114), kind=kOutput, calls=%fused_computation | convolution fusion | flops 2819260416 | bytes 13434884 | tf_op jit(solution)/shard_map/dot_general | solution.py:272
  204.2 0.6 collective-permute-start.11
  204.8 2.8 %collective-permute-done.11 = bf16[256,2688]{1,0:T(8,128)(2,1)S(1)} collective-permute-done((bf16[256,2688]{1,0:T(8,128)(2,1)S(1)}, bf16[256,2688]{1,0:T(8,128)(2,1)S(1)}, u32[]{:S(2)}, u32[]{:S(2)}) %collective-permute-start.11) | collective-permute-done | bytes 1376288 | tf_op jit(solution)/shard_map/ppermute | solution.py:274
  207.5 8.7 %fusion.2 = bf16[256,2688]{1,0:T(8,128)(2,1)} fusion(bf16[2048,2688]{1,0:T(8,128)(2,1)} %param.9, bf16[256,2688]{1,0:T(8,128)(2,1)S(1)} %collective-permute-done.11, bf16[512,2048]{1,0:T(8,128)(2,1)} %get-tuple-element.11, s32[]{:T(128)S(6)} %select_n.113), kind=kOutput, calls=%fused_computation.4 | convolution fusion | flops 2822012928 | bytes 14811140 | tf_op jit(solution)/shard_map/dot_general | solution.py:272
  (11 shorter events, 0.2 us)
Async XLA Ops:
  0.6 18.6 %copy-start = (f32[8,128,64]{1,2,0:T(8,128)S(1)}, f32[8,128,64]{1,2,0:T(8,128)}, u32[]{:S(2)}) copy-start(f32[8,128,64]{1,2,0:T(8,128)} %param.8) | copy-start | bytes 786436
  0.7 1.3 copy-start.1
  2.5 7.2 %collective-permute-start = (f32[4,128,128]{2,1,0:T(8,128)S(1)}, f32[4,128,128]{2,1,0:T(8,128)S(1)}, u32[]{:S(2)}, u32[]{:S(2)}) collective-permute-start(f32[4,128,128]{2,1,0:T(8,128)S(1)} %slice_select_fusion), channel_id=1, source_target_pairs={{0,2},{2,0},{4,6},{6,4},{8,10},{10,8},{12,14},{14,12},{16,18},{18,... | collective-permute-start | bytes 786440 | tf_op jit(solution)/shard_map/ppermute | solution.py:133
  9.8 3.9 %collective-permute-start.1 = (f32[2,128,128]{2,1,0:T(8,128)S(1)}, f32[2,128,128]{2,1,0:T(8,128)S(1)}, u32[]{:S(2)}, u32[]{:S(2)}) collective-permute-start(f32[2,128,128]{2,1,0:T(8,128)S(1)} %slice_select_fusion.1), channel_id=1, source_target_pairs={{0,4},{2,6},{4,0},{6,2},{8,12},{10,14},{12,8},{14,10},{16,20},{18,... | collective-permute-start | bytes 393224 | tf_op jit(solution)/shard_map/ppermute | solution.py:133
  13.7 3.2 %collective-permute-start.2 = (f32[1,128,128]{2,1,0:T(8,128)S(1)}, f32[1,128,128]{2,1,0:T(8,128)S(1)}, u32[]{:S(2)}, u32[]{:S(2)}) collective-permute-start(f32[1,128,128]{2,1,0:T(8,128)S(1)} %slice_select_fusion.2), channel_id=1, source_target_pairs={{0,8},{2,10},{4,12},{6,14},{8,0},{10,2},{12,4},{14,6},{16,24},{18,... | collective-permute-start | bytes 196616 | tf_op jit(solution)/shard_map/ppermute | solution.py:133
  16.9 4.7 %collective-permute-start.3 = (f32[1,128,128]{2,1,0:T(8,128)S(1)}, f32[1,128,128]{2,1,0:T(8,128)S(1)}, u32[]{:S(2)}, u32[]{:S(2)}) collective-permute-start(f32[1,128,128]{2,1,0:T(8,128)S(1)} %select_add_fusion.2), channel_id=1, source_target_pairs={{0,16},{2,18},{4,20},{6,22},{8,24},{10,26},{12,28},{14,30},{16,0},... | collective-permute-start | bytes 196616 | tf_op jit(solution)/shard_map/ppermute | solution.py:133
  21.6 28.2 %copy-start.2 = (bf16[512,1024]{1,0:T(8,128)(2,1)S(1)}, bf16[512,1024]{1,0:T(8,128)(2,1)}, u32[]{:S(2)}) copy-start(bf16[512,1024]{1,0:T(8,128)(2,1)} %refs_3_) | copy-start | bytes 3145732
  49.8 12.9 %collective-permute-start.8 = (bf16[1,128,64]{2,1,0:T(8,128)(2,1)S(1)}, bf16[1,128,64]{2,1,0:T(8,128)(2,1)S(1)}, u32[]{:S(2)}, u32[]{:S(2)}) collective-permute-start(bf16[1,128,64]{2,1,0:T(8,128)(2,1)S(1)} %basis.1), channel_id=1, source_target_pairs={{0,8},{2,10},{4,12},{6,14},{8,0},{10,2},{12,4},{14,6},{16,24},{18,... | collective-permute-start | bytes 49160 | tf_op jit(solution)/shard_map/ppermute | solution.py:133
  49.9 108.6 %collective-permute-start.4 = (bf16[512,1024]{1,0:T(8,128)(2,1)S(1)}, bf16[512,1024]{1,0:T(8,128)(2,1)S(1)}, u32[]{:S(2)}, u32[]{:S(2)}) collective-permute-start(bf16[512,1024]{1,0:T(8,128)(2,1)S(1)} %copy-done.2), channel_id=1, source_target_pairs={{0,4},{2,6},{4,8},{6,10},{8,12},{10,14},{12,16},{14,18},{16,20},{1... | collective-permute-start | bytes 3145736 | tf_op jit(solution)/shard_map/ppermute | solution.py:31
  54.2 104.2 %collective-permute-start.5 = (bf16[512,1024]{1,0:T(8,128)(2,1)S(1)}, bf16[512,1024]{1,0:T(8,128)(2,1)S(1)}, u32[]{:S(2)}, u32[]{:S(2)}) collective-permute-start(bf16[512,1024]{1,0:T(8,128)(2,1)S(1)} %copy-done.2), channel_id=1, source_target_pairs={{0,2},{2,4},{4,6},{6,8},{8,10},{10,12},{12,14},{14,16},{16,18},{18... | collective-permute-start | bytes 3145736 | tf_op jit(solution)/shard_map/ppermute | solution.py:31
  57.4 101.1 %collective-permute-start.6 = (bf16[512,1024]{1,0:T(8,128)(2,1)}, bf16[512,1024]{1,0:T(8,128)(2,1)}, u32[]{:S(2)}, u32[]{:S(2)}) collective-permute-start(bf16[512,1024]{1,0:T(8,128)(2,1)} %refs_6_), channel_id=1, source_target_pairs={{0,4},{2,6},{4,8},{6,10},{8,12},{10,14},{12,16},{14,18},{16,20},{1... | collective-permute-start | bytes 3145736 | tf_op jit(solution)/shard_map/ppermute | solution.py:31
  60.5 97.9 %collective-permute-start.7 = (bf16[512,1024]{1,0:T(8,128)(2,1)}, bf16[512,1024]{1,0:T(8,128)(2,1)}, u32[]{:S(2)}, u32[]{:S(2)}) collective-permute-start(bf16[512,1024]{1,0:T(8,128)(2,1)} %refs_6_), channel_id=1, source_target_pairs={{0,2},{2,4},{4,6},{6,8},{8,10},{10,12},{12,14},{14,16},{16,18},{18... | collective-permute-start | bytes 3145736 | tf_op jit(solution)/shard_map/ppermute | solution.py:31
  62.7 77.7 %collective-permute-start.9 = (bf16[2,128,64]{2,1,0:T(8,128)(2,1)S(1)}, bf16[2,128,64]{2,1,0:T(8,128)(2,1)S(1)}, u32[]{:S(2)}, u32[]{:S(2)}) collective-permute-start(bf16[2,128,64]{2,1,0:T(8,128)(2,1)S(1)} %pad_maximum_fusion.2), channel_id=1, source_target_pairs={{0,4},{2,6},{4,0},{6,2},{8,12},{10,14},{12,8},{14,10},{16,20},{18,... | collective-permute-start | bytes 98312 | tf_op jit(solution)/shard_map/ppermute | solution.py:133
  141.1 16.3 %collective-permute-start.10 = (bf16[4,128,64]{2,1,0:T(8,128)(2,1)}, bf16[4,128,64]{2,1,0:T(8,128)(2,1)}, u32[]{:S(2)}, u32[]{:S(2)}) collective-permute-start(bf16[4,128,64]{2,1,0:T(8,128)(2,1)} %pad_maximum_fusion.1), channel_id=1, source_target_pairs={{0,2},{2,0},{4,6},{6,4},{8,10},{10,8},{12,14},{14,12},{16,18},{18,... | collective-permute-start | bytes 196616 | tf_op jit(solution)/shard_map/ppermute | solution.py:133
  204.2 3.3 %collective-permute-start.11 = (bf16[256,2688]{1,0:T(8,128)(2,1)S(1)}, bf16[256,2688]{1,0:T(8,128)(2,1)S(1)}, u32[]{:S(2)}, u32[]{:S(2)}) collective-permute-start(bf16[256,2688]{1,0:T(8,128)(2,1)S(1)} %convolution_convert_fusion), channel_id=1, source_target_pairs={{0,1},{1,0},{2,3},{3,2},{4,5},{5,4},{6,7},{7,6},{8,9},{9,8},{10,11... | collective-permute-start | bytes 4128776 | tf_op jit(solution)/shard_map/ppermute | solution.py:274

commit v3 on v2

--- a/solution.py
+++ b/solution.py
@@ -202,6 +202,9 @@
         ),
         name="gram",
     )(keys)
+    far = [
+        (from_behind(keys, "seq", d), from_behind(values, "seq", d)) for d in range(prior, 1, -1)
+    ]
     peers = lax.axis_size("seq")
     where_at = lax.axis_index("seq")
     spread = peers >= heads and peers & (peers - 1) == 0 and heads & (heads - 1) == 0
@@ -216,11 +219,10 @@
             else:
                 total = total + partner(total, "seq", bit)
             bit *= 2
-        total, keys, values = lax.optimization_barrier((total, keys, values))
     else:
         total = lax.psum(local_gram, "seq")
-    key_blocks = [from_behind(keys, "seq", d) for d in range(prior, 0, -1)] + [keys]
-    value_blocks = [from_behind(values, "seq", d) for d in range(prior, 0, -1)] + [values]
+    total, keys, values, far = lax.optimization_barrier((total, keys, values, far))
+    near = (from_behind(keys, "seq", 1), from_behind(values, "seq", 1))
     if spread:
         owner, left, bit = 0, heads, 1
         while left > 1:
@@ -229,6 +231,7 @@
             bit *= 2
         start = lax.dynamic_slice_in_dim(start_basis, owner, 1, 0)
         basis_half = subspace(total, start)
+        basis_half, near = lax.optimization_barrier((basis_half, near))
         while bit > 1:
             bit //= 2
             upper = (where_at & bit) != 0
@@ -238,6 +241,9 @@
             )
     else:
         basis_half = subspace(total, start_basis)
+
+    blocks = far + [near, (keys, values)]
+    key_blocks, value_blocks = [b[0] for b in blocks], [b[1] for b in blocks]
 
     wide = pl.BlockSpec((tok_rows, GROUP * HD), lambda h: (0, h))
     narrow = pl.BlockSpec((tok_rows, HD), lambda h: (0, h))

time: 216 us -> 193 us (0.89); the launches traced: 216 us -> 190 us
  waiting for transfers between devices: 110 us -> 69.5 us
  starting transfers between devices: 19 us -> 29.7 us
  local copies, waits for them, and re-layouts: 1.37 us -> 5.75 us
    ppermute x7, waiting for transfers between devices: 107 us -> 57.3 us  [partner(): lax.ppermute(array, axis, [(i, i ^ mask) for i in range(lax.axis_size(axi...]
    ppermute x4, waiting for transfers between devices: 0.01 us -> 9.18 us  [from_behind(): return lax.ppermute(array, axis, pairs)]
    ppermute x1, starting transfers between devices: 0.55 us -> 7.14 us  [shards(): arrived = lax.ppermute(project(1 - mine), 'head', [(0, 1), (1, 0)])]
    unnamed x7 -> x15, local copies, waits for them, and re-layouts: 1.37 us -> 5.74 us
    ppermute x7, starting transfers between devices: 5.75 us -> 8.12 us  [partner(): lax.ppermute(array, axis, [(i, i ^ mask) for i in range(lax.axis_size(axi...]
  transfers between devices with their start and end apart: 12 -> 12, of which waited for: 7 -> 8; matrix products, arithmetic and copies ran while one was open for 1% -> 0% of each run, Pallas kernels for 0% -> 15%
where the time goes in v3:
time: 193 us; the launch traced here: 190 us
  waiting for transfers between devices  69.5 us (36%)
  Pallas kernels  66.8 us (35%)
  starting transfers between devices  29.7 us (15%)
  matrix products  17.4 us (9%)
  local copies, waits for them, and re-layouts  5.75 us (3%)
    ppermute x7, waiting for transfers between devices, partner(): lax.ppermute(array, axis, [(i, i ^ mask) for i in range(lax.axis_size(axi...  57.3 us
    pallas_call x1, Pallas kernels, shards(): pl.pallas_call(functools.partial(attend_kernel, prior), grid=(heads,), in...  38.2 us
    pallas_call x1, Pallas kernels, subspace(): pl.pallas_call(basis_kernel, grid=(heads,), in_specs=[pl.BlockSpec((1, HD...  28.1 us
    dot_general x2, matrix products, project(): return jnp.dot(rows, out_weight, preferred_element_type=F32).astype(BF16)  17.4 us
    ppermute x4, starting transfers between devices, from_behind(): return lax.ppermute(array, axis, pairs)  14.5 us
    ppermute x4, waiting for transfers between devices, from_behind(): return lax.ppermute(array, axis, pairs)  9.18 us
    ppermute x7, starting transfers between devices, partner(): lax.ppermute(array, axis, [(i, i ^ mask) for i in range(lax.axis_size(axi...  8.12 us
    ppermute x1, starting transfers between devices, shards(): arrived = lax.ppermute(project(1 - mine), 'head', [(0, 1), (1, 0)])  7.14 us
  transfers between devices with their start and end apart: 12, of which 8 were waited for; matrix products, arithmetic and copies ran while one was open for 0% of the time, Pallas kernels for 15%

profile of v3, /device:TPU:13, one launch (start us, length us, event | category | flops | bytes accessed | tf_op | source)
XLA Modules:
  0.0 190.3 jit_solution(16185295961490533502)
XLA Ops:
  0.6 0.0 copy-start
  0.7 0.0 copy-start.1
  0.7 1.3 copy-done.1
  1.9 0.0 copy-start.2
  1.9 0.5 gram.1
  2.5 1.3 collective-permute-start
  3.7 0.0 copy-done.2
  3.7 3.1 %collective-permute-start.4 = (bf16[512,1024]{1,0:T(8,128)(2,1)S(1)}, bf16[512,1024]{1,0:T(8,128)(2,1)S(1)}, u32[]{:S(2)}, u32[]{:S(2)}) collective-permute-start(bf16[512,1024]{1,0:T(8,128)(2,1)S(1)} %copy-done.2), channel_id=1, source_target_pairs={{0,4},{2,6},{4,8},{6,10},{8,12},{10,14},{12,16},{14,18},{16,20},{1... | collective-permute-start | bytes 3145736 | tf_op jit(solution)/shard_map/ppermute | solution.py:31
  6.9 3.1 %collective-permute-start.5 = (bf16[512,1024]{1,0:T(8,128)(2,1)}, bf16[512,1024]{1,0:T(8,128)(2,1)}, u32[]{:S(2)}, u32[]{:S(2)}) collective-permute-start(bf16[512,1024]{1,0:T(8,128)(2,1)} %refs_6_), channel_id=1, source_target_pairs={{0,4},{2,6},{4,8},{6,10},{8,12},{10,14},{12,16},{14,18},{16,20},{1... | collective-permute-start | bytes 3145736 | tf_op jit(solution)/shard_map/ppermute | solution.py:31
  10.0 0.0 collective-permute-done
  10.1 0.3 collective-permute-start.1
  10.4 44.5 %collective-permute-done.1 = f32[2,128,128]{2,1,0:T(8,128)S(1)} collective-permute-done((f32[2,128,128]{2,1,0:T(8,128)S(1)}, f32[2,128,128]{2,1,0:T(8,128)S(1)}, u32[]{:S(2)}, u32[]{:S(2)}) %collective-permute-start.1) | collective-permute-done | bytes 131104 | tf_op jit(solution)/shard_map/ppermute | solution.py:133
  54.9 0.1 collective-permute-start.2
  55.0 3.1 %collective-permute-done.2 = f32[1,128,128]{2,1,0:T(8,128)S(1)} collective-permute-done((f32[1,128,128]{2,1,0:T(8,128)S(1)}, f32[1,128,128]{2,1,0:T(8,128)S(1)}, u32[]{:S(2)}, u32[]{:S(2)}) %collective-permute-start.2) | collective-permute-done | bytes 65568 | tf_op jit(solution)/shard_map/ppermute | solution.py:133
  58.1 2.4 %collective-permute-start.3 = (f32[1,128,128]{2,1,0:T(8,128)S(1)}, f32[1,128,128]{2,1,0:T(8,128)S(1)}, u32[]{:S(2)}, u32[]{:S(2)}) collective-permute-start(f32[1,128,128]{2,1,0:T(8,128)S(1)} %select_add_fusion.2), channel_id=1, source_target_pairs={{0,16},{2,18},{4,20},{6,22},{8,24},{10,26},{12,28},{14,30},{16,0},... | collective-permute-start | bytes 196616 | tf_op jit(solution)/shard_map/ppermute | solution.py:133
  60.5 0.0 copy-done
  60.5 0.1 copy.8.start_ref
  60.6 1.7 collective-permute-done.3
  62.3 0.0 collective-permute-done.4.refs_1_
  62.3 0.0 collective-permute-done.5.refs_4_
  62.4 2.5 %collective-permute-start.6 = (bf16[512,1024]{1,0:T(8,128)(2,1)S(1)}, bf16[512,1024]{1,0:T(8,128)(2,1)S(1)}, u32[]{:S(2)}, u32[]{:S(2)}) collective-permute-start(bf16[512,1024]{1,0:T(8,128)(2,1)S(1)} %copy-done.2), channel_id=1, source_target_pairs={{0,2},{2,4},{4,6},{6,8},{8,10},{10,12},{12,14},{14,16},{16,18},{18... | collective-permute-start | bytes 3145736 | tf_op jit(solution)/shard_map/ppermute | solution.py:31
  64.9 5.6 %collective-permute-start.7 = (bf16[512,1024]{1,0:T(8,128)(2,1)}, bf16[512,1024]{1,0:T(8,128)(2,1)S(1)}, u32[]{:S(2)}, u32[]{:S(2)}) collective-permute-start(bf16[512,1024]{1,0:T(8,128)(2,1)} %refs_6_), channel_id=1, source_target_pairs={{0,2},{2,4},{4,6},{6,8},{8,10},{10,12},{12,14},{14,16},{16,18},{18... | collective-permute-start | bytes 3145736 | tf_op jit(solution)/shard_map/ppermute | solution.py:31
  70.6 28.1 %basis.1 = bf16[1,128,64]{2,1,0:T(8,128)(2,1)S(1)} custom-call(f32[1,128,128]{2,1,0:T(8,128)S(1)} %add.33.gram_ref, f32[1,128,64]{2,1,0:T(8,128)S(1)} %copy.8.start_ref), custom_call_target="tpu_custom_call" | custom-call | flops 40000000000 | bytes 2097152 | tf_op jit(solution)/shard_map/basis/pallas_call | solution.py:114
  98.7 0.0 collective-permute-done.6.refs_2_
  98.7 0.0 copy-start.3
  98.7 1.0 copy-done.3
  99.7 9.2 %collective-permute-done.7.refs_5_ = bf16[512,1024]{1,0:T(8,128)(2,1)S(1)} collective-permute-done((bf16[512,1024]{1,0:T(8,128)(2,1)}, bf16[512,1024]{1,0:T(8,128)(2,1)S(1)}, u32[]{:S(2)}, u32[]{:S(2)}) %collective-permute-start.7) | collective-permute-done | bytes 1048608 | tf_op jit(solution)/shard_map/ppermute | solution.py:31
  108.9 0.0 copy-start.5
  108.9 1.0 copy-done.5
  109.8 0.4 collective-permute-start.8
  110.2 2.7 %collective-permute-done.8 = bf16[1,128,64]{2,1,0:T(8,128)(2,1)S(1)} collective-permute-done((bf16[1,128,64]{2,1,0:T(8,128)(2,1)S(1)}, bf16[1,128,64]{2,1,0:T(8,128)(2,1)S(1)}, u32[]{:S(2)}, u32[]{:S(2)}) %collective-permute-start.8) | collective-permute-done | bytes 16416 | tf_op jit(solution)/shard_map/ppermute | solution.py:133
  112.9 3.6 %collective-permute-start.9 = (bf16[2,128,64]{2,1,0:T(8,128)(2,1)S(1)}, bf16[2,128,64]{2,1,0:T(8,128)(2,1)S(1)}, u32[]{:S(2)}, u32[]{:S(2)}) collective-permute-start(bf16[2,128,64]{2,1,0:T(8,128)(2,1)S(1)} %pad_maximum_fusion.2), channel_id=1, source_target_pairs={{0,4},{2,6},{4,0},{6,2},{8,12},{10,14},{12,8},{14,10},{16,20},{18,... | collective-permute-start | bytes 98312 | tf_op jit(solution)/shard_map/ppermute | solution.py:133
  116.5 1.7 collective-permute-done.9
  118.2 0.1 collective-permute-start.10
  118.3 3.8 %collective-permute-done.10 = bf16[4,128,64]{2,1,0:T(8,128)(2,1)S(1)} collective-permute-done((bf16[4,128,64]{2,1,0:T(8,128)(2,1)S(1)}, bf16[4,128,64]{2,1,0:T(8,128)(2,1)S(1)}, u32[]{:S(2)}, u32[]{:S(2)}) %collective-permute-start.10) | collective-permute-done | bytes 65568 | tf_op jit(solution)/shard_map/ppermute | solution.py:133
  122.2 0.1 pad_maximum_fusion.refs_7_
  122.2 0.0 copy-start.4
  122.2 1.2 copy-done.4
  123.4 0.0 copy-start.6
  123.4 1.2 copy-done.6
  124.7 38.2 %attend.1 = (bf16[512,2048]{1,0:T(8,128)(2,1)}, bf16[512,2048]{1,0:T(8,128)(2,1)}) custom-call(bf16[512,2048]{1,0:T(8,128)(2,1)} %refs_0_.1, bf16[512,1024]{1,0:T(8,128)(2,1)S(1)} %collective-permute-done.4.refs_1_, bf16[512,1024]{1,0:T(8,128)(2,1)S(1)} %copy-done.4, bf16[512,1024]{1,0:T(8,128)(2,1)S(1)} %copy-done.2, ...), custom_call_target="tpu_custom_call" | custom-call | flops 30000001024 | bytes 16777216 | tf_op jit(solution)/shard_map/attend/pallas_call | solution.py:251
  162.8 8.7 %convolution_convert_fusion = bf16[256,2688]{1,0:T(8,128)(2,1)} fusion(bf16[2048,2688]{1,0:T(8,128)(2,1)} %param.9, bf16[512,2048]{1,0:T(8,128)(2,1)} %get-tuple-element.21, s32[]{:T(128)S(6)} %select_n.114), kind=kOutput, calls=%fused_computation | convolution fusion | flops 2819260416 | bytes 13434884 | tf_op jit(solution)/shard_map/dot_general | solution.py:278
  171.5 7.1 %collective-permute-start.11 = (bf16[256,2688]{1,0:T(8,128)(2,1)}, bf16[256,2688]{1,0:T(8,128)(2,1)S(1)}, u32[]{:S(2)}, u32[]{:S(2)}) collective-permute-start(bf16[256,2688]{1,0:T(8,128)(2,1)} %convolution_convert_fusion), channel_id=1, source_target_pairs={{0,1},{1,0},{2,3},{3,2},{4,5},{5,4},{6,7},{7,6},{8,9},{9,8},{10,11... | collective-permute-start | bytes 4128776 | tf_op jit(solution)/shard_map/ppermute | solution.py:280
  178.7 3.0 %collective-permute-done.11 = bf16[256,2688]{1,0:T(8,128)(2,1)S(1)} collective-permute-done((bf16[256,2688]{1,0:T(8,128)(2,1)}, bf16[256,2688]{1,0:T(8,128)(2,1)S(1)}, u32[]{:S(2)}, u32[]{:S(2)}) %collective-permute-start.11) | collective-permute-done | bytes 1376288 | tf_op jit(solution)/shard_map/ppermute | solution.py:280
  181.6 8.7 %add_convert_fusion = bf16[256,2688]{1,0:T(8,128)(2,1)} fusion(bf16[256,2688]{1,0:T(8,128)(2,1)S(1)} %collective-permute-done.11, bf16[2048,2688]{1,0:T(8,128)(2,1)} %param.9, bf16[512,2048]{1,0:T(8,128)(2,1)} %get-tuple-element.21, s32[]{:T(128)S(6)} %select_n.113), kind=kOutput, calls=%fused_computation.3 | convolution fusion | flops 2822012928 | bytes 14811140 | tf_op jit(solution)/shard_map/dot_general | solution.py:278
  (13 shorter events, 0.3 us)
Async XLA Ops:
  0.6 59.9 %copy-start = (f32[8,128,64]{1,2,0:T(8,128)S(1)}, f32[8,128,64]{1,2,0:T(8,128)}, u32[]{:S(2)}) copy-start(f32[8,128,64]{1,2,0:T(8,128)} %param.8) | copy-start | bytes 786436
  0.7 1.3 copy-start.1
  1.9 1.8 copy-start.2
  2.5 7.6 %collective-permute-start = (f32[4,128,128]{2,1,0:T(8,128)S(1)}, f32[4,128,128]{2,1,0:T(8,128)S(1)}, u32[]{:S(2)}, u32[]{:S(2)}) collective-permute-start(f32[4,128,128]{2,1,0:T(8,128)S(1)} %slice_select_fusion), channel_id=1, source_target_pairs={{0,2},{2,0},{4,6},{6,4},{8,10},{10,8},{12,14},{14,12},{16,18},{18,... | collective-permute-start | bytes 786440 | tf_op jit(solution)/shard_map/ppermute | solution.py:133
  3.7 58.6 %collective-permute-start.4 = (bf16[512,1024]{1,0:T(8,128)(2,1)S(1)}, bf16[512,1024]{1,0:T(8,128)(2,1)S(1)}, u32[]{:S(2)}, u32[]{:S(2)}) collective-permute-start(bf16[512,1024]{1,0:T(8,128)(2,1)S(1)} %copy-done.2), channel_id=1, source_target_pairs={{0,4},{2,6},{4,8},{6,10},{8,12},{10,14},{12,16},{14,18},{16,20},{1... | collective-permute-start | bytes 3145736 | tf_op jit(solution)/shard_map/ppermute | solution.py:31
  6.9 55.5 %collective-permute-start.5 = (bf16[512,1024]{1,0:T(8,128)(2,1)}, bf16[512,1024]{1,0:T(8,128)(2,1)}, u32[]{:S(2)}, u32[]{:S(2)}) collective-permute-start(bf16[512,1024]{1,0:T(8,128)(2,1)} %refs_6_), channel_id=1, source_target_pairs={{0,4},{2,6},{4,8},{6,10},{8,12},{10,14},{12,16},{14,18},{16,20},{1... | collective-permute-start | bytes 3145736 | tf_op jit(solution)/shard_map/ppermute | solution.py:31
  10.1 44.8 %collective-permute-start.1 = (f32[2,128,128]{2,1,0:T(8,128)S(1)}, f32[2,128,128]{2,1,0:T(8,128)S(1)}, u32[]{:S(2)}, u32[]{:S(2)}) collective-permute-start(f32[2,128,128]{2,1,0:T(8,128)S(1)} %slice_select_fusion.1), channel_id=1, source_target_pairs={{0,4},{2,6},{4,0},{6,2},{8,12},{10,14},{12,8},{14,10},{16,20},{18,... | collective-permute-start | bytes 393224 | tf_op jit(solution)/shard_map/ppermute | solution.py:133
  54.9 3.2 %collective-permute-start.2 = (f32[1,128,128]{2,1,0:T(8,128)S(1)}, f32[1,128,128]{2,1,0:T(8,128)S(1)}, u32[]{:S(2)}, u32[]{:S(2)}) collective-permute-start(f32[1,128,128]{2,1,0:T(8,128)S(1)} %slice_select_fusion.2), channel_id=1, source_target_pairs={{0,8},{2,10},{4,12},{6,14},{8,0},{10,2},{12,4},{14,6},{16,24},{18,... | collective-permute-start | bytes 196616 | tf_op jit(solution)/shard_map/ppermute | solution.py:133
  58.1 4.2 %collective-permute-start.3 = (f32[1,128,128]{2,1,0:T(8,128)S(1)}, f32[1,128,128]{2,1,0:T(8,128)S(1)}, u32[]{:S(2)}, u32[]{:S(2)}) collective-permute-start(f32[1,128,128]{2,1,0:T(8,128)S(1)} %select_add_fusion.2), channel_id=1, source_target_pairs={{0,16},{2,18},{4,20},{6,22},{8,24},{10,26},{12,28},{14,30},{16,0},... | collective-permute-start | bytes 196616 | tf_op jit(solution)/shard_map/ppermute | solution.py:133
  62.4 36.3 %collective-permute-start.6 = (bf16[512,1024]{1,0:T(8,128)(2,1)S(1)}, bf16[512,1024]{1,0:T(8,128)(2,1)S(1)}, u32[]{:S(2)}, u32[]{:S(2)}) collective-permute-start(bf16[512,1024]{1,0:T(8,128)(2,1)S(1)} %copy-done.2), channel_id=1, source_target_pairs={{0,2},{2,4},{4,6},{6,8},{8,10},{10,12},{12,14},{14,16},{16,18},{18... | collective-permute-start | bytes 3145736 | tf_op jit(solution)/shard_map/ppermute | solution.py:31
  64.9 43.9 %collective-permute-start.7 = (bf16[512,1024]{1,0:T(8,128)(2,1)}, bf16[512,1024]{1,0:T(8,128)(2,1)S(1)}, u32[]{:S(2)}, u32[]{:S(2)}) collective-permute-start(bf16[512,1024]{1,0:T(8,128)(2,1)} %refs_6_), channel_id=1, source_target_pairs={{0,2},{2,4},{4,6},{6,8},{8,10},{10,12},{12,14},{14,16},{16,18},{18... | collective-permute-start | bytes 3145736 | tf_op jit(solution)/shard_map/ppermute | solution.py:31
  98.7 1.0 copy-start.3
  108.9 1.0 copy-start.5
  109.8 3.1 %collective-permute-start.8 = (bf16[1,128,64]{2,1,0:T(8,128)(2,1)S(1)}, bf16[1,128,64]{2,1,0:T(8,128)(2,1)S(1)}, u32[]{:S(2)}, u32[]{:S(2)}) collective-permute-start(bf16[1,128,64]{2,1,0:T(8,128)(2,1)S(1)} %basis.1), channel_id=1, source_target_pairs={{0,8},{2,10},{4,12},{6,14},{8,0},{10,2},{12,4},{14,6},{16,24},{18,... | collective-permute-start | bytes 49160 | tf_op jit(solution)/shard_map/ppermute | solution.py:133
  112.9 5.2 %collective-permute-start.9 = (bf16[2,128,64]{2,1,0:T(8,128)(2,1)S(1)}, bf16[2,128,64]{2,1,0:T(8,128)(2,1)S(1)}, u32[]{:S(2)}, u32[]{:S(2)}) collective-permute-start(bf16[2,128,64]{2,1,0:T(8,128)(2,1)S(1)} %pad_maximum_fusion.2), channel_id=1, source_target_pairs={{0,4},{2,6},{4,0},{6,2},{8,12},{10,14},{12,8},{14,10},{16,20},{18,... | collective-permute-start | bytes 98312 | tf_op jit(solution)/shard_map/ppermute | solution.py:133
  118.2 3.9 %collective-permute-start.10 = (bf16[4,128,64]{2,1,0:T(8,128)(2,1)S(1)}, bf16[4,128,64]{2,1,0:T(8,128)(2,1)S(1)}, u32[]{:S(2)}, u32[]{:S(2)}) collective-permute-start(bf16[4,128,64]{2,1,0:T(8,128)(2,1)S(1)} %pad_maximum_fusion.1), channel_id=1, source_target_pairs={{0,2},{2,0},{4,6},{6,4},{8,10},{10,8},{12,14},{14,12},{16,18},{18,... | collective-permute-start | bytes 196616 | tf_op jit(solution)/shard_map/ppermute | solution.py:133
  122.2 1.2 copy-start.4
  123.4 1.2 copy-start.6
  171.5 10.1 %collective-permute-start.11 = (bf16[256,2688]{1,0:T(8,128)(2,1)}, bf16[256,2688]{1,0:T(8,128)(2,1)S(1)}, u32[]{:S(2)}, u32[]{:S(2)}) collective-permute-start(bf16[256,2688]{1,0:T(8,128)(2,1)} %convolution_convert_fusion), channel_id=1, source_target_pairs={{0,1},{1,0},{2,3},{3,2},{4,5},{5,4},{6,7},{7,6},{8,9},{9,8},{10,11... | collective-permute-start | bytes 4128776 | tf_op jit(solution)/shard_map/ppermute | solution.py:280
